TPU v7x, 128 devices: a whole 4x4x4 slice. The times are simulated.
128 devices in a mesh: fsdp: 4 (over x), heads: 8 (over z, core), tensor: 4 (over y).
Axes of the slice: x: 4, y: 4, z: 4, core: 2. Of those that a mesh axis runs over, the one named last changes fastest.
Arguments:
- hidden_in: bfloat16 [8, 4, 512, 1024], P('fsdp', 'tensor', 'heads'), may hold values from -6 to 6
- cotangent: bfloat16 [8, 4, 512, 1024], P('fsdp', 'tensor', 'heads'), may hold values from -6 to 6
- block_order: int32 [4, 2], replicated, may hold values from 0 to 7, as said below
- query_weight: bfloat16 [1024, 8, 128], P(('fsdp', 'tensor'), 'heads'), may hold values from -0.1875 to 0.1875
- keyval_weight: bfloat16 [1024, 8, 128], P(('fsdp', 'tensor'), 'heads'), may hold values from -0.1875 to 0.1875
- output_weight: bfloat16 [1024, 8, 128], P(('fsdp', 'tensor'), 'heads'), may hold values from -1.5 to 1.5
- gate_weight: bfloat16 [1024, 4608], P(('fsdp', 'heads'), 'tensor'), may hold values from -0.1875 to 0.1875
- up_weight: bfloat16 [1024, 4608], P(('fsdp', 'heads'), 'tensor'), may hold values from -0.1875 to 0.1875
- down_weight: bfloat16 [1024, 4608], P(('fsdp', 'heads'), 'tensor'), may hold values from -0.09375 to 0.09375
- attn_gain: float32 [1024], replicated, may hold values from 0.1 to 1.9
- ffn_gain: float32 [1024], replicated, may hold values from 0.1 to 1.9
- query_gain: float32 [64], replicated, may hold values from 0.1 to 1.9
- key_gain: float32 [64], replicated, may hold values from 0.1 to 1.9
Outputs:
- block_out: bfloat16 [8, 4, 512, 1024], P('fsdp', 'tensor', 'heads')
- input_grad: float32 [8, 4, 512, 1024], P('fsdp', 'tensor', 'heads')
- query_grad: float32 [1024, 8, 128], P(('fsdp', 'tensor'), 'heads')
- keyval_grad: float32 [1024, 8, 128], P(('fsdp', 'tensor'), 'heads')
- output_grad: float32 [1024, 8, 128], P(('fsdp', 'tensor'), 'heads')
- gate_grad: float32 [1024, 4608], P(('fsdp', 'heads'), 'tensor')
- up_grad: float32 [1024, 4608], P(('fsdp', 'heads'), 'tensor')
- down_grad: float32 [1024, 4608], P(('fsdp', 'heads'), 'tensor')
- attn_gain_grad: float32 [1024], replicated
- ffn_gain_grad: float32 [1024], replicated
- query_gain_grad: float32 [64], replicated
- key_gain_grad: float32 [64], replicated
Inputs may be any that keep to these rules, and one draw needn't show every extreme that they name: `block_order`: row r holds the two query blocks that tensor rank r keeps: a block c of 0 to 2 n - 1 (n the tensor axis's devices) and its mirror 2 n - 1 - c, in either order; every block appears exactly once.
All inputs are finite; a program needn't handle non-finite values.
Results may differ from a plain program's by a relative error of at most 0.019.
Values may be sent and summed in bfloat16 or wider, within the bound.
No kernel may reach another device: no remote copies, remote signals or barrier semaphores. Data moves between devices by JAX's collectives and lax.ppermute only.
A program may use at most 128 MiB of HBM per device.

v0:
```python
import jax
import jax.numpy as jnp
from jax import lax
from jax.sharding import PartitionSpec as P

eps_norm = 1e-05
rope_base = 1000000.0
masked_value = -1e30


def rms_scale(values):
    return lax.rsqrt(jnp.mean(values * values, axis=-1, keepdims=True) + eps_norm)


def rope_tables(positions, head_width):
    half = head_width // 2
    freq = rope_base ** (-(jnp.arange(half, dtype=jnp.float32) * 2.0 / head_width))
    angles = positions.astype(jnp.float32)[:, None] * freq[None, :]
    return (jnp.cos(angles), jnp.sin(angles))


def rotate(values, cosine, sine):
    half = values.shape[-1] // 2
    first = values[..., :half]
    second = values[..., half:]
    return jnp.concatenate(
        [first * cosine - second * sine, second * cosine + first * sine], axis=-1
    )


def rotate_back(grads, cosine, sine):
    half = grads.shape[-1] // 2
    first = grads[..., :half]
    second = grads[..., half:]
    return jnp.concatenate(
        [first * cosine + second * sine, second * cosine - first * sine], axis=-1
    )


def norm_back(values, scale, gain, grads):
    scaled = grads * gain
    inner = jnp.mean(scaled * values, axis=-1, keepdims=True)
    return (scale * (scaled - values * scale * scale * inner), grads * values * scale)


def matmul(left, right):
    return jnp.dot(left, right, preferred_element_type=jnp.float32)


def contract_rows(left, right):
    return lax.dot_general(
        left, right, (((0,), (0,)), ((), ())), preferred_element_type=jnp.float32
    )


def contract_cols(left, right):
    return lax.dot_general(
        left, right, (((1,), (1,)), ((), ())), preferred_element_type=jnp.float32
    )


def masked_scores(queries, keys, query_pos, key_pos, scale):
    scores = jnp.einsum("ckgd,lkd->kgcl", queries, keys, preferred_element_type=jnp.float32) * scale
    allowed = query_pos[:, None] >= key_pos[None, :]
    return jnp.where(allowed[None, None], scores, masked_value)


def attend(queries, keys, values, query_pos, key_pos, scale):
    scores = masked_scores(queries, keys, query_pos, key_pos, scale)
    row_max = jnp.max(scores, axis=-1, keepdims=True)
    raised = jnp.exp(scores - row_max)
    total = jnp.sum(raised, axis=-1, keepdims=True)
    shares = (raised / total).astype(jnp.bfloat16)
    context = jnp.einsum("kgcl,lkd->ckgd", shares, values, preferred_element_type=jnp.float32)
    return (context.astype(jnp.bfloat16), (row_max + jnp.log(total))[..., 0])


def attend_back(queries, keys, values, logsum, context_grad, query_pos, key_pos, scale):
    scores = masked_scores(queries, keys, query_pos, key_pos, scale)
    shares = jnp.exp(scores - logsum[..., None])
    share_grad = jnp.einsum(
        "ckgd,lkd->kgcl", context_grad, values, preferred_element_type=jnp.float32
    )
    share_dot = jnp.sum(shares * share_grad, axis=-1, keepdims=True)
    score_low = (shares * (share_grad - share_dot)).astype(jnp.bfloat16)
    query_part = (
        jnp.einsum("kgcl,lkd->ckgd", score_low, keys, preferred_element_type=jnp.float32) * scale
    )
    key_part = (
        jnp.einsum("kgcl,ckgd->lkd", score_low, queries, preferred_element_type=jnp.float32) * scale
    )
    value_part = jnp.einsum(
        "kgcl,ckgd->lkd",
        shares.astype(jnp.bfloat16),
        context_grad,
        preferred_element_type=jnp.float32,
    )
    return (query_part, key_part, value_part)


def gather_attention(query_weight, keyval_weight, output_weight):
    return (
        lax.all_gather(query_weight, ("fsdp", "tensor"), axis=0, tiled=True),
        lax.all_gather(keyval_weight, ("fsdp", "tensor"), axis=0, tiled=True),
        lax.all_gather(output_weight, ("fsdp", "tensor"), axis=0, tiled=True),
    )


def gather_feed(gate_weight, up_weight, down_weight):
    return (
        lax.all_gather(gate_weight, ("fsdp", "heads"), axis=0, tiled=True),
        lax.all_gather(up_weight, ("fsdp", "heads"), axis=0, tiled=True),
        lax.all_gather(down_weight, ("fsdp", "heads"), axis=0, tiled=True),
    )


def body(
    hidden_in,
    cotangent,
    block_order,
    query_weight,
    keyval_weight,
    output_weight,
    gate_weight,
    up_weight,
    down_weight,
    attn_gain,
    ffn_gain,
    query_gain,
    key_gain,
):
    sequences = hidden_in.shape[0]
    own_rows = hidden_in.shape[2]
    width = hidden_in.shape[3]
    tensor_size = lax.axis_size("tensor")
    heads_size = lax.axis_size("heads")
    shard_rows = own_rows * heads_size
    block_len = shard_rows // 2
    seq_len = shard_rows * tensor_size
    head_dim = query_gain.shape[0]
    kv_heads = query_weight.shape[1]
    query_width = query_weight.shape[2]
    group_size = query_width // head_dim
    scale = head_dim ** (-0.5)
    own_blocks = lax.dynamic_slice_in_dim(block_order, lax.axis_index("tensor"), 1, 0)[0]
    offsets = jnp.arange(block_len, dtype=jnp.int32)
    query_pos = own_blocks[:, None] * block_len + offsets[None, :]
    key_pos = (block_order[:, :, None] * block_len + offsets[None, None, :]).reshape(seq_len)
    cosine, sine = rope_tables(query_pos.reshape(shard_rows), head_dim)
    cos_query = cosine[None, :, None, None, :]
    sin_query = sine[None, :, None, None, :]
    cos_key = cosine[None, :, None, :]
    sin_key = sine[None, :, None, :]
    query_all, keyval_all, output_all = gather_attention(query_weight, keyval_weight, output_weight)
    query_flat = query_all.reshape(width, kv_heads * query_width)
    keyval_flat = keyval_all.reshape(width, kv_heads * 2 * head_dim)
    output_flat = output_all.reshape(width, kv_heads * query_width)
    inputs = hidden_in.astype(jnp.float32)
    scale_one = rms_scale(inputs)
    normed_one = (inputs * scale_one * attn_gain).astype(jnp.bfloat16)
    rows_all = lax.all_gather(normed_one, "heads", axis=2, tiled=True)
    rows_flat = rows_all.reshape(sequences * shard_rows, width)
    query_raw = matmul(rows_flat, query_flat).reshape(
        sequences, shard_rows, kv_heads, group_size, head_dim
    )
    keyval_raw = matmul(rows_flat, keyval_flat).reshape(
        sequences, shard_rows, kv_heads, 2, head_dim
    )
    key_raw = keyval_raw[:, :, :, 0]
    value_raw = keyval_raw[:, :, :, 1]
    query_scale = rms_scale(query_raw)
    key_scale = rms_scale(key_raw)
    query_rot = rotate(query_raw * query_scale * query_gain, cos_query, sin_query).astype(
        jnp.bfloat16
    )
    key_rot = rotate(key_raw * key_scale * key_gain, cos_key, sin_key).astype(jnp.bfloat16)
    sending = jnp.stack([key_rot, value_raw.astype(jnp.bfloat16)], axis=3)
    sending = sending.reshape(sequences, 1, shard_rows, kv_heads, 2 * head_dim)
    gathered = lax.all_gather(sending, "tensor", axis=1, tiled=True)
    gathered = gathered.reshape(sequences, seq_len, kv_heads, 2, head_dim)
    keys_all = gathered[:, :, :, 0]
    values_all = gathered[:, :, :, 1]
    query_slots = query_rot.reshape(sequences, 2, block_len, kv_heads, group_size, head_dim)

    def forward_sequence(operands):
        seq_queries, seq_keys, seq_values = operands
        contexts = []
        logsums = []
        for slot in range(2):
            context, logsum = attend(
                seq_queries[slot], seq_keys, seq_values, query_pos[slot], key_pos, scale
            )
            contexts.append(context)
            logsums.append(logsum)
        return (jnp.stack(contexts), jnp.stack(logsums))

    contexts, logsums = lax.map(forward_sequence, (query_slots, keys_all, values_all))
    context_flat = contexts.reshape(sequences * shard_rows, kv_heads * query_width)
    branch_part = contract_cols(context_flat, output_flat).reshape(sequences, 1, shard_rows, width)
    branch = lax.psum_scatter(branch_part, "heads", scatter_dimension=2, tiled=True)
    middle = inputs + branch
    scale_two = rms_scale(middle)
    normed_two = (middle * scale_two * ffn_gain).astype(jnp.bfloat16)
    rows_two, cot_rows = (
        lax.all_gather(normed_two, "tensor", axis=1, tiled=True),
        lax.all_gather(cotangent, "tensor", axis=1, tiled=True),
    )
    two_flat = rows_two.reshape(sequences * tensor_size * own_rows, width)
    cot_flat = cot_rows.reshape(sequences * tensor_size * own_rows, width)
    gate_all, up_all, down_all = gather_feed(gate_weight, up_weight, down_weight)
    gate_value = matmul(two_flat, gate_all)
    upper_value = matmul(two_flat, up_all)
    sigmoid_gate = jax.nn.sigmoid(gate_value)
    activated = gate_value * sigmoid_gate
    hidden = (activated * upper_value).astype(jnp.bfloat16)
    feed_part = contract_cols(hidden, down_all).reshape(sequences, tensor_size, own_rows, width)
    feed = lax.psum_scatter(
        feed_part.astype(jnp.bfloat16), "tensor", scatter_dimension=1, tiled=True
    ).astype(jnp.float32)
    block_out = (middle + feed).astype(jnp.bfloat16)
    gate_back, up_back, down_back = gather_feed(gate_weight, up_weight, down_weight)
    hidden_grad = matmul(cot_flat, down_back)
    down_grad = contract_rows(cot_flat, hidden)
    gate_low = (
        hidden_grad * upper_value * sigmoid_gate * (1.0 + gate_value * (1.0 - sigmoid_gate))
    ).astype(jnp.bfloat16)
    upper_low = (hidden_grad * activated).astype(jnp.bfloat16)
    gate_grad = contract_rows(two_flat, gate_low)
    up_grad = contract_rows(two_flat, upper_low)
    normed_two_part = contract_cols(gate_low, gate_back) + contract_cols(upper_low, up_back)
    normed_two_part = normed_two_part.reshape(sequences, tensor_size, own_rows, width)
    normed_two_grad = lax.psum_scatter(normed_two_part, "tensor", scatter_dimension=1, tiled=True)
    feed_grads = (
        lax.psum_scatter(
            gate_grad.astype(jnp.bfloat16), ("fsdp", "heads"), scatter_dimension=0, tiled=True
        ).astype(jnp.float32),
        lax.psum_scatter(
            up_grad.astype(jnp.bfloat16), ("fsdp", "heads"), scatter_dimension=0, tiled=True
        ).astype(jnp.float32),
        lax.psum_scatter(
            down_grad.astype(jnp.bfloat16), ("fsdp", "heads"), scatter_dimension=0, tiled=True
        ).astype(jnp.float32),
    )
    middle_norm_grad, ffn_terms = norm_back(middle, scale_two, ffn_gain, normed_two_grad)
    middle_grad = cotangent.astype(jnp.float32) + middle_norm_grad
    branch_low = middle_grad.astype(jnp.bfloat16)
    branch_all = lax.all_gather(branch_low, "heads", axis=2, tiled=True)
    branch_flat = branch_all.reshape(sequences * shard_rows, width)
    query_back, keyval_back, output_back = gather_attention(
        query_weight, keyval_weight, output_weight
    )
    query_back = query_back.reshape(width, kv_heads * query_width)
    keyval_back = keyval_back.reshape(width, kv_heads * 2 * head_dim)
    output_back = output_back.reshape(width, kv_heads * query_width)
    context_grad = matmul(branch_flat, output_back).astype(jnp.bfloat16)
    output_grad = contract_rows(branch_flat, context_flat).reshape(width, kv_heads, query_width)
    context_slots = context_grad.reshape(sequences, 2, block_len, kv_heads, group_size, head_dim)

    def backward_sequence(operands):
        seq_queries, seq_keys, seq_values, seq_logsums, seq_grads = operands
        key_total = jnp.zeros((seq_len, kv_heads, head_dim), jnp.float32)
        value_total = jnp.zeros((seq_len, kv_heads, head_dim), jnp.float32)
        query_parts = []
        for slot in range(2):
            query_part, key_part, value_part = attend_back(
                seq_queries[slot],
                seq_keys,
                seq_values,
                seq_logsums[slot],
                seq_grads[slot],
                query_pos[slot],
                key_pos,
                scale,
            )
            query_parts.append(query_part)
            key_total = key_total + key_part
            value_total = value_total + value_part
        return (jnp.stack(query_parts), key_total, value_total)

    query_rot_grad, key_terms_all, value_terms_all = lax.map(
        backward_sequence, (query_slots, keys_all, values_all, logsums, context_slots)
    )
    kv_terms = jnp.stack([key_terms_all, value_terms_all], axis=3)
    kv_terms = kv_terms.reshape(sequences, tensor_size, shard_rows, kv_heads, 2 * head_dim)
    kv_own = lax.psum_scatter(kv_terms, "tensor", scatter_dimension=1, tiled=True)
    kv_own = kv_own.reshape(sequences, shard_rows, kv_heads, 2, head_dim)
    key_rot_grad = kv_own[:, :, :, 0]
    value_grad = kv_own[:, :, :, 1]
    query_rot_grad = query_rot_grad.reshape(sequences, shard_rows, kv_heads, group_size, head_dim)
    query_norm_grad = rotate_back(query_rot_grad, cos_query, sin_query)
    query_raw_grad, query_terms = norm_back(query_raw, query_scale, query_gain, query_norm_grad)
    key_norm_grad = rotate_back(key_rot_grad, cos_key, sin_key)
    key_raw_grad, key_terms = norm_back(key_raw, key_scale, key_gain, key_norm_grad)
    query_low = query_raw_grad.astype(jnp.bfloat16).reshape(
        sequences * shard_rows, kv_heads * query_width
    )
    keyval_low = jnp.stack([key_raw_grad, value_grad], axis=3).astype(jnp.bfloat16)
    keyval_low = keyval_low.reshape(sequences * shard_rows, kv_heads * 2 * head_dim)
    normed_one_part = contract_cols(query_low, query_back) + contract_cols(keyval_low, keyval_back)
    normed_one_part = normed_one_part.reshape(sequences, 1, shard_rows, width)
    normed_one_grad = lax.psum_scatter(
        normed_one_part.astype(jnp.bfloat16), "heads", scatter_dimension=2, tiled=True
    ).astype(jnp.float32)
    query_grad = contract_rows(rows_flat, query_low).reshape(width, kv_heads, query_width)
    keyval_grad = contract_rows(rows_flat, keyval_low).reshape(width, kv_heads, 2 * head_dim)
    attn_grads = (
        lax.psum_scatter(
            query_grad.astype(jnp.bfloat16), ("fsdp", "tensor"), scatter_dimension=0, tiled=True
        ).astype(jnp.float32),
        lax.psum_scatter(
            keyval_grad.astype(jnp.bfloat16), ("fsdp", "tensor"), scatter_dimension=0, tiled=True
        ).astype(jnp.float32),
        lax.psum_scatter(
            output_grad.astype(jnp.bfloat16), ("fsdp", "tensor"), scatter_dimension=0, tiled=True
        ).astype(jnp.float32),
    )
    input_norm_grad, attn_terms = norm_back(inputs, scale_one, attn_gain, normed_one_grad)
    input_grad = middle_grad + input_norm_grad
    gains = lax.psum(
        (
            jnp.sum(attn_terms, axis=(0, 1, 2)),
            jnp.sum(ffn_terms, axis=(0, 1, 2)),
            jnp.sum(query_terms, axis=(0, 1, 2, 3)),
            jnp.sum(key_terms, axis=(0, 1, 2)),
        ),
        ("fsdp", "heads", "tensor"),
    )
    return (
        block_out,
        input_grad,
        attn_grads[0],
        attn_grads[1],
        attn_grads[2],
        feed_grads[0],
        feed_grads[1],
        feed_grads[2],
        gains[0],
        gains[1],
        gains[2],
        gains[3],
    )


def solution(mesh):
    placed = (
        P("fsdp", "tensor", "heads", None),
        P("fsdp", "tensor", "heads", None),
        P(),
        P(("fsdp", "tensor"), "heads", None),
        P(("fsdp", "tensor"), "heads", None),
        P(("fsdp", "tensor"), "heads", None),
        P(("fsdp", "heads"), "tensor"),
        P(("fsdp", "heads"), "tensor"),
        P(("fsdp", "heads"), "tensor"),
        P(),
        P(),
        P(),
        P(),
    )
    return jax.shard_map(
        body,
        mesh=mesh,
        in_specs=placed,
        out_specs=(
            P("fsdp", "tensor", "heads", None),
            P("fsdp", "tensor", "heads", None),
            P(("fsdp", "tensor"), "heads", None),
            P(("fsdp", "tensor"), "heads", None),
            P(("fsdp", "tensor"), "heads", None),
            P(("fsdp", "heads"), "tensor"),
            P(("fsdp", "heads"), "tensor"),
            P(("fsdp", "heads"), "tensor"),
            P(),
            P(),
            P(),
            P(),
        ),
        check_vma=False,
    )
```

profile of v0, /device:TPU:24, one launch (start us, length us, event | category | flops | bytes accessed | tf_op | source)
XLA Modules:
  0.0 1056.0 jit_solution(298240113666964048)
XLA Ops:
  11.1 23.4 %all_gather.40 = bf16[1024,1,128]{2,0,1:T(8,128)(2,1)S(1)} all-gather(bf16[64,1,128]{2,0,1:T(8,128)(2,1)} %param.21), channel_id=1, replica_groups=mesh['fsdp'=4,'heads'=8,'tensor'=4] {'fsdp','tensor'}, dimensions={0}, use_global_device_ids=true | all-gather | bytes 278528 | tf_op jit(solution)/shard_map/all_gather | solution.py:104
  42.0 23.6 %all_gather.42 = bf16[1024,1,128]{2,0,1:T(8,128)(2,1)S(1)} all-gather(bf16[64,1,128]{2,0,1:T(8,128)(2,1)S(1)} %copy-done.41), channel_id=1, replica_groups=mesh['fsdp'=4,'heads'=8,'tensor'=4] {'fsdp','tensor'}, dimensions={0}, use_global_device_ids=true | all-gather | bytes 278528 | tf_op jit(solution)/shard_map/all_gather | solution.py:103
  65.8 21.7 %all_gather.43 = bf16[1024,1,128]{2,0,1:T(8,128)(2,1)S(1)} all-gather(bf16[64,1,128]{2,0,1:T(8,128)(2,1)S(1)} %copy-done.42), channel_id=1, replica_groups=mesh['fsdp'=4,'heads'=8,'tensor'=4] {'fsdp','tensor'}, dimensions={0}, use_global_device_ids=true | all-gather | bytes 278528 | tf_op jit(solution)/shard_map/all_gather | solution.py:105
  96.1 12.0 %while.28 = (s32[]{:T(128)}, bf16[2,2,256,1,2,64]{2,5,4,1,3,0:T(8,128)(2,1)}, f32[2,2,1,2,256]{4,3,1,2,0:T(2,128)S(1)}, bf16[2,2048,1,64]{1,3,2,0:T(8,128)(2,1)S...) while((s32[]{:T(128)}, ...), condition=%wide.region_8.9_spmd.clone, body=%wide.region_3.8_spmd.clone.sunk | while | flops 555026432 | bytes 31015656 | solution.py:197
  112.4 38.2 %reduce-scatter.14.cloned.1.call-done = f32[2,1,64,1024]{3,2,0,1:T(8,128)} async-done(((f32[2,1,512,1024]{3,2,0,1:T(8,128)}), f32[2,1,64,1024]{3,2,0,1:T(8,128)}) %reduce-scatter.14.cloned.1.call-update) | async-done | bytes 524304 | tf_op jit(solution)/shard_map/reduce_scatter | solution.py:200
  155.5 18.8 %all-gather.13.cloned.1.call-done = bf16[2,4,64,1024]{3,2,0,1:T(8,128)(2,1)} async-done(((bf16[2,1,64,1024]{3,2,0,1:T(8,128)(2,1)}), bf16[2,4,64,1024]{3,2,0,1:T(8,128)(2,1)}) %all-gather.13.cloned.1.call-update) | async-done | bytes 1048592 | tf_op jit(solution)/shard_map/all_gather | solution.py:205
  175.7 46.4 %all-gather.17.cloned.1.call-done = bf16[1024,1152]{1,0:T(8,128)(2,1)} async-done(((bf16[32,1152]{1,0:T(8,128)(2,1)}), bf16[1024,1152]{1,0:T(8,128)(2,1)}) %all-gather.17.cloned.1.call-update) | async-done | bytes 2359312 | tf_op jit(solution)/shard_map/all_gather | solution.py:112
  222.1 4.6 fusion.139
  226.7 41.1 %all-gather.15.cloned.1.call-done = bf16[1024,1152]{1,0:T(8,128)(2,1)} async-done(((bf16[32,1152]{1,0:T(8,128)(2,1)}), bf16[1024,1152]{1,0:T(8,128)(2,1)}) %all-gather.15.cloned.1.call-update) | async-done | bytes 2359312 | tf_op jit(solution)/shard_map/all_gather | solution.py:111
  267.8 4.7 fusion.138
  272.5 19.3 %all-gather.21.cloned.1.call-done = bf16[2,4,64,1024]{3,2,1,0:T(8,128)(2,1)} async-done(((bf16[2,1,64,1024]{3,2,1,0:T(8,128)(2,1)}), bf16[2,4,64,1024]{3,2,1,0:T(8,128)(2,1)}) %all-gather.21.cloned.1.call-update) | async-done | bytes 1048592 | tf_op jit(solution)/shard_map/all_gather | solution.py:206
  291.8 47.9 %all-gather.19.cloned.1.call-done = bf16[1024,1152]{1,0:T(8,128)(2,1)} async-done(((bf16[32,1152]{1,0:T(8,128)(2,1)}), bf16[1024,1152]{1,0:T(8,128)(2,1)}) %all-gather.19.cloned.1.call-update) | async-done | bytes 2359312 | tf_op jit(solution)/shard_map/all_gather | solution.py:113
  339.7 6.7 multiply_convert_fusion
  352.0 27.2 %reduce-scatter.18.cloned.1.call-done = f32[2,1,64,1024]{3,2,0,1:T(8,128)} async-done(((f32[2,4,64,1024]{3,2,0,1:T(8,128)}), f32[2,1,64,1024]{3,2,0,1:T(8,128)}) %reduce-scatter.18.cloned.1.call-update) | async-done | bytes 524304 | tf_op jit(solution)/shard_map/reduce_scatter | solution.py:232
  382.9 26.7 %all-gather.23.cloned.1.call-done = bf16[2,1,512,1024]{3,2,0,1:T(8,128)(2,1)} async-done(((bf16[2,1,64,1024]{3,2,0,1:T(8,128)(2,1)}), bf16[2,1,512,1024]{3,2,0,1:T(8,128)(2,1)}) %all-gather.23.cloned.1.call-update) | async-done | bytes 2097168 | tf_op jit(solution)/shard_map/all_gather | solution.py:247
  412.5 26.5 %while.29 = (s32[]{:T(128)}, f32[2,2,256,1,2,64]{2,1,0,5,4,3:T(2,128)}, f32[2,2048,1,64]{1,3,2,0:T(8,128)}, f32[2,2048,1,64]{1,3,2,0:T(8,128)}, bf16[2,2048,1,64...) while((s32[]{:T(128)}, ...), condition=%wide.region_17.18_spmd.clone, body=%wide.region_14.17_spmd.clone.sunk | while | flops 1362625536 | bytes 92604800 | solution.py:280
  496.8 62.2 %reduce-scatter.34.cloned.1.call-done = bf16[32,1152]{1,0:T(8,128)(2,1)} async-done(((bf16[1024,1152]{1,0:T(8,128)(2,1)}), bf16[32,1152]{1,0:T(8,128)(2,1)}) %reduce-scatter.34.cloned.1.call-update) | async-done | bytes 73744
  561.0 80.8 %reduce-scatter.32.cloned.1.call-done = bf16[32,1152]{1,0:T(8,128)(2,1)} async-done(((bf16[1024,1152]{1,0:T(8,128)(2,1)}), bf16[32,1152]{1,0:T(8,128)(2,1)}) %reduce-scatter.32.cloned.1.call-update) | async-done | bytes 73744 | tf_op jit(solution)/shard_map/reduce_scatter | solution.py:237
  643.3 80.5 %reduce-scatter.30.cloned.1.call-done = bf16[32,1152]{1,0:T(8,128)(2,1)} async-done(((bf16[1024,1152]{1,0:T(8,128)(2,1)}), bf16[32,1152]{1,0:T(8,128)(2,1)}) %reduce-scatter.30.cloned.1.call-update) | async-done | bytes 73744 | tf_op jit(solution)/shard_map/reduce_scatter | solution.py:234
  725.5 72.5 %reduce-scatter.28.cloned.1.call-done = bf16[64,1,128]{2,0,1:T(8,128)(2,1)} async-done(((bf16[1024,1,128]{2,0,1:T(8,128)(2,1)}), bf16[64,1,128]{2,0,1:T(8,128)(2,1)}) %reduce-scatter.28.cloned.1.call-update) | async-done | bytes 16400 | tf_op jit(solution)/shard_map/reduce_scatter | solution.py:313
  799.3 73.0 %reduce-scatter.24.cloned.1.call-done = bf16[64,1,128]{2,0,1:T(8,128)(2,1)} async-done(((bf16[1024,1,128]{2,0,1:T(8,128)(2,1)}), bf16[64,1,128]{2,0,1:T(8,128)(2,1)}) %reduce-scatter.24.cloned.1.call-update) | async-done | bytes 16400 | tf_op jit(solution)/shard_map/reduce_scatter | solution.py:307
  873.6 73.3 %reduce-scatter.26.cloned.1.call-done = bf16[64,1,128]{2,0,1:T(8,128)(2,1)} async-done(((bf16[1024,1,128]{2,0,1:T(8,128)(2,1)}), bf16[64,1,128]{2,0,1:T(8,128)(2,1)}) %reduce-scatter.26.cloned.1.call-update) | async-done | bytes 16400 | tf_op jit(solution)/shard_map/reduce_scatter | solution.py:310
  948.2 34.6 %reduce-scatter.22.cloned.1.call-done = bf16[2,1,64,1024]{3,2,0,1:T(8,128)(2,1)} async-done(((bf16[2,1,512,1024]{3,2,0,1:T(8,128)(2,1)}), bf16[2,1,64,1024]{3,2,0,1:T(8,128)(2,1)}) %reduce-scatter.22.cloned.1.call-update) | async-done | bytes 262160 | tf_op jit(solution)/shard_map/reduce_scatter | solution.py:301
  984.0 63.0 %all-reduce = (f32[1024]{0:T(1024)}, f32[1024]{0:T(1024)}, f32[64]{0:T(128)}, f32[64]{0:T(128)}) all-reduce(f32[1024]{0:T(1024)S(1)} %get-tuple-element.283, f32[1024]{0:T(1024)S(1)} %get-tuple-element.279, f32[64]{0:T(128)S(1)} %reduce_sum.163, ...), channel_id=1, replica_groups=mesh['fsdp'=4,'heads'=8,'tensor'=4] {'fsdp','heads','tensor'}, use_global_device_ids=true, to_apply=%region_30.31 | all-reduce | flops 2176 | bytes 17408 | tf_op jit(solution)/shard_map/psum | solution.py:319
  (345 shorter events, 150.5 us)
Async XLA Ops:
  7.2 30.7 %all-gather.9.cloned.1.call-start = ((), (), s32[]{:S(2)}) async-start(), calls=%async_computation.11 | async-start | bytes 2359296 | tf_op jit(solution)/shard_map/all_gather | solution.py:161
  10.1 83.2 %all-gather.11.cloned.1.call-start = ((), (), s32[]{:S(2)}) async-start(), calls=%async_computation.12 | async-start | bytes 1310720 | tf_op jit(solution)/shard_map/all_gather | solution.py:179
  42.0 108.6 %reduce-scatter.14.cloned.1.call-start = ((), (), s32[]{:S(2)}) async-start(), calls=%async_computation.13 | async-start | bytes 4718592 | tf_op jit(solution)/shard_map/reduce_scatter | solution.py:200
  112.3 62.0 %all-gather.13.cloned.1.call-start = ((), (), s32[]{:S(2)}) async-start(), calls=%async_computation.14 | async-start | bytes 1310720 | tf_op jit(solution)/shard_map/all_gather | solution.py:205
  152.6 69.4 %all-gather.17.cloned.1.call-start = ((), (), s32[]{:S(2)}) async-start(), calls=%async_computation.16 | async-start | bytes 2433024 | tf_op jit(solution)/shard_map/all_gather | solution.py:112
  153.2 114.6 %all-gather.15.cloned.1.call-start = ((), (), s32[]{:S(2)}) async-start(), calls=%async_computation.15 | async-start | bytes 2433024 | tf_op jit(solution)/shard_map/all_gather | solution.py:111
  153.8 138.0 %all-gather.21.cloned.1.call-start = ((), (), s32[]{:S(2)}) async-start(), calls=%async_computation.19 | async-start | bytes 1310720 | tf_op jit(solution)/shard_map/all_gather | solution.py:206
  154.5 185.1 %all-gather.19.cloned.1.call-start = ((), (), s32[]{:S(2)}) async-start(), calls=%async_computation.17 | async-start | bytes 2433024 | tf_op jit(solution)/shard_map/all_gather | solution.py:113
  155.3 223.9 %reduce-scatter.18.cloned.1.call-start = ((), (), s32[]{:S(2)}) async-start(), calls=%async_computation.20 | async-start | bytes 2621440 | tf_op jit(solution)/shard_map/reduce_scatter | solution.py:232
  352.0 57.6 %all-gather.23.cloned.1.call-start = ((), (), s32[]{:S(2)}) async-start(), calls=%async_computation.21 | async-start | bytes 2359296 | tf_op jit(solution)/shard_map/all_gather | solution.py:247
  382.4 98.2 %reduce-scatter.20.cloned.1.call-start = ((), (), s32[]{:S(2)}) async-start(), calls=%async_computation.22 | async-start | bytes 2621440 | tf_op jit(solution)/shard_map/reduce_scatter | solution.py:285
  446.3 112.7 %reduce-scatter.34.cloned.1.call-start = ((), (), s32[]{:S(2)}) async-start(), calls=%async_computation.29 | async-start | bytes 2433024
  452.0 189.8 %reduce-scatter.32.cloned.1.call-start = ((), (), s32[]{:S(2)}) async-start(), calls=%async_computation.28 | async-start | bytes 2433024 | tf_op jit(solution)/shard_map/reduce_scatter | solution.py:237
  456.5 267.3 %reduce-scatter.30.cloned.1.call-start = ((), (), s32[]{:S(2)}) async-start(), calls=%async_computation.27 | async-start | bytes 2433024 | tf_op jit(solution)/shard_map/reduce_scatter | solution.py:234
  460.8 337.2 %reduce-scatter.28.cloned.1.call-start = ((), (), s32[]{:S(2)}) async-start(), calls=%async_computation.26 | async-start | bytes 278528 | tf_op jit(solution)/shard_map/reduce_scatter | solution.py:313
  471.5 400.7 %reduce-scatter.24.cloned.1.call-start = ((), (), s32[]{:S(2)}) async-start(), calls=%async_computation.24 | async-start | bytes 278528 | tf_op jit(solution)/shard_map/reduce_scatter | solution.py:307
  480.6 466.3 %reduce-scatter.26.cloned.1.call-start = ((), (), s32[]{:S(2)}) async-start(), calls=%async_computation.25 | async-start | bytes 278528 | tf_op jit(solution)/shard_map/reduce_scatter | solution.py:310
  488.3 494.5 %reduce-scatter.22.cloned.1.call-start = ((), (), s32[]{:S(2)}) async-start(), calls=%async_computation.23 | async-start | bytes 2359296 | tf_op jit(solution)/shard_map/reduce_scatter | solution.py:301
  492.1 554.9 %reduce-scatter.16.cloned.1.call-start = ((), (), s32[]{:S(2)}) async-start(), calls=%async_computation.18 | async-start | bytes 1310720 | tf_op jit(solution)/shard_map/reduce_scatter | solution.py:217
  495.7 487.1 %copy-start.3 = (bf16[2,1,64,1024]{3,2,1,0:T(8,128)(2,1)S(1)}, bf16[2,1,64,1024]{3,2,1,0:T(8,128)(2,1)}, u32[]{:S(2)}) copy-start(bf16[2,1,64,1024]{3,2,1,0:T(8,128)(2,1)} %param.17) | copy-start | bytes 786436
  495.7 487.1 %copy-start.38 = (f32[1024]{0:T(1024)S(1)}, f32[1024]{0:T(1024)}, u32[]{:S(2)}) copy-start(f32[1024]{0:T(1024)} %param.26) | copy-start | bytes 12292
  495.7 487.1 %copy-start.40 = (f32[2,64]{1,0:T(2,128)S(1)}, f32[2,64]{1,0:T(2,128)}, u32[]{:S(2)}) copy-start(f32[2,64]{1,0:T(2,128)} %copy-done.39) | copy-start | bytes 1540
  495.7 551.3 %copy-start.4 = (f32[2,1,64,1024]{3,2,0,1:T(8,128)S(1)}, f32[2,1,64,1024]{3,2,0,1:T(8,128)}, u32[]{:S(2)}) copy-start(f32[2,1,64,1024]{3,2,0,1:T(8,128)} %reduce-scatter.18.cloned.1.call-done) | copy-start | bytes 1572868
  495.7 551.3 %copy-start.44 = (f32[2,64]{1,0:T(2,128)S(1)}, f32[2,64]{1,0:T(2,128)}, u32[]{:S(2)}) copy-start(f32[2,64]{1,0:T(2,128)} %copy-done.43) | copy-start | bytes 1540
  (61 other events, 837.8 us)
Sparse Core Ops, SparseCore 0:
  10.3 27.5 all-gather.8
  42.1 23.6 all-gather.10
  112.4 38.0 reduce-scatter.13
  152.7 21.5 all-gather.12
  176.4 45.5 all-gather.16
  224.2 43.5 all-gather.14
  269.4 22.2 all-gather.20
  294.0 45.5 all-gather.18
  352.1 27.0 reduce-scatter.17
  382.5 26.9 all-gather.22
  446.4 28.1 reduce-scatter.19
  478.1 80.9 reduce-scatter.33
  563.0 78.6 reduce-scatter.31
  645.2 78.6 reduce-scatter.29
  727.2 70.7 reduce-scatter.27
  801.0 71.2 reduce-scatter.23
  875.6 71.2 reduce-scatter.25
  949.2 33.6 reduce-scatter.21
  985.2 20.1 reduce-scatter.15
where the time goes:
time: 1060 us
  waiting for transfers between devices  748 us (71%)
  blocking collectives  132 us (12%)
  matrix products  73.4 us (7%)
  local copies, waits for them, and re-layouts  48.4 us (5%)
  other arithmetic  37.3 us (4%)
  between operations  15 us (1%)
    reduce_scatter x1, waiting for transfers between devices, body(): lax.psum_scatter(up_grad.astype(jnp.bfloat16), ('fsdp', 'heads'), scatter...  80.8 us
    reduce_scatter x1, waiting for transfers between devices, body(): lax.psum_scatter(gate_grad.astype(jnp.bfloat16), ('fsdp', 'heads'), scatt...  80.5 us
    reduce_scatter x1, waiting for transfers between devices, body(): lax.psum_scatter(keyval_grad.astype(jnp.bfloat16), ('fsdp', 'tensor'), sc...  73.3 us
    reduce_scatter x1, waiting for transfers between devices, body(): lax.psum_scatter(query_grad.astype(jnp.bfloat16), ('fsdp', 'tensor'), sca...  73 us
    reduce_scatter x1, waiting for transfers between devices, body(): lax.psum_scatter(output_grad.astype(jnp.bfloat16), ('fsdp', 'tensor'), sc...  72.5 us
    unnamed x20, waiting for transfers between devices  64.9 us
    psum x1, blocking collectives, body(): lax.psum((jnp.sum(attn_terms, axis=(0, 1, 2)), jnp.sum(ffn_terms, axis=(0...  63 us
    all_gather x1, waiting for transfers between devices, gather_feed(): lax.all_gather(down_weight, ('fsdp', 'heads'), axis=0, tiled=True)  47.9 us
  transfers between devices with their start and end apart: 19, of which 16 were waited for; matrix products, arithmetic and copies ran while one was open for 7% of the time, Pallas kernels for 0%

commit v1 on v0

v1 whole, which is shorter than its diff:
```python
import jax
import jax.numpy as jnp
from jax import lax
from jax.sharding import PartitionSpec as P

eps_norm = 1e-05
rope_base = 1000000.0
masked_value = -1e30


def rms_scale(values):
    return lax.rsqrt(jnp.mean(values * values, axis=-1, keepdims=True) + eps_norm)


def rope_tables(positions, head_width):
    half = head_width // 2
    freq = rope_base ** (-(jnp.arange(half, dtype=jnp.float32) * 2.0 / head_width))
    angles = positions.astype(jnp.float32)[:, None] * freq[None, :]
    return (jnp.cos(angles), jnp.sin(angles))


def rotate(values, cosine, sine):
    half = values.shape[-1] // 2
    first = values[..., :half]
    second = values[..., half:]
    return jnp.concatenate(
        [first * cosine - second * sine, second * cosine + first * sine], axis=-1
    )


def rotate_back(grads, cosine, sine):
    half = grads.shape[-1] // 2
    first = grads[..., :half]
    second = grads[..., half:]
    return jnp.concatenate(
        [first * cosine + second * sine, second * cosine - first * sine], axis=-1
    )


def norm_back(values, scale, gain, grads):
    scaled = grads * gain
    inner = jnp.mean(scaled * values, axis=-1, keepdims=True)
    return (scale * (scaled - values * scale * scale * inner), grads * values * scale)


def matmul(left, right):
    return jnp.dot(left, right, preferred_element_type=jnp.float32)


def contract_rows(left, right):
    return lax.dot_general(
        left, right, (((0,), (0,)), ((), ())), preferred_element_type=jnp.float32
    )


def contract_cols(left, right):
    return lax.dot_general(
        left, right, (((1,), (1,)), ((), ())), preferred_element_type=jnp.float32
    )


def sum_four(parts):
    return (parts[0] + parts[2]) + (parts[1] + parts[3])


def shift_chips(values, axis, step):
    size = lax.axis_size(axis)
    return lax.ppermute(values, axis, [(i, (i + step) % size) for i in range(size)])


def shift_z(values, step):
    size = lax.axis_size("heads")
    return lax.ppermute(values, "heads", [(i, (i + 2 * step) % size) for i in range(size)])


def swap_core(values):
    size = lax.axis_size("heads")
    return lax.ppermute(values, "heads", [(i, i ^ 1) for i in range(size)])


def gather_ring(values, axis):
    shift = shift_z if axis == "z" else lambda v, s: shift_chips(v, axis, s)
    return [values] + [shift(values, s) for s in (1, 2, 3)]


def scatter_ring(parts, axis):
    shift = shift_z if axis == "z" else lambda v, s: shift_chips(v, axis, s)
    return [parts[0]] + [shift(parts[s], -s) for s in (1, 2, 3)]


def gather_heads(values):
    own = jnp.stack(gather_ring(values, "z"))
    return jnp.stack([own, swap_core(own)])


def scatter_heads(parts):
    own = parts[0].astype(jnp.float32) + swap_core(parts[1]).astype(jnp.float32)
    own_low = own.astype(jnp.bfloat16)
    moved = scatter_ring([own[0], own_low[1], own_low[2], own_low[3]], "z")
    return sum_four([part.astype(jnp.float32) for part in moved])


def scatter_tensor(parts, first):
    moved = scatter_ring([first, parts[1], parts[2], parts[3]], "tensor")
    return sum_four([part.astype(jnp.float32) for part in moved])


def reduce_all(values):
    values = values + swap_core(values)
    for axis in ("z", "tensor", "fsdp"):
        values = sum_four(gather_ring(values, axis))
    return values


def scatter_rows(grads, axis):
    size = lax.axis_size(axis)
    rank = lax.axis_index(axis)
    rows = grads.shape[0] // size
    pieces = [
        lax.dynamic_slice_in_dim(grads, lax.rem(rank - s + size, size) * rows, rows, 0)
        for s in range(size)
    ]
    moved = scatter_ring([pieces[0]] + [p.astype(jnp.bfloat16) for p in pieces[1:]], axis)
    return sum_four([part.astype(jnp.float32) for part in moved])


def masked_scores(queries, keys, query_pos, key_pos, scale):
    scores = jnp.einsum("cgd,ld->gcl", queries, keys, preferred_element_type=jnp.float32) * scale
    allowed = query_pos[:, None] >= key_pos[None, :]
    return jnp.where(allowed[None], scores, masked_value)


def attend(queries, keys, values, query_pos, key_pos, scale):
    scores = masked_scores(queries, keys, query_pos, key_pos, scale)
    row_max = jnp.max(scores, axis=-1, keepdims=True)
    raised = jnp.exp(scores - row_max)
    total = jnp.sum(raised, axis=-1, keepdims=True)
    shares = (raised / total).astype(jnp.bfloat16)
    context = jnp.einsum("gcl,ld->cgd", shares, values, preferred_element_type=jnp.float32)
    return (context.astype(jnp.bfloat16), (row_max + jnp.log(total))[..., 0])


def attend_back(queries, keys, values, logsum, context_grad, query_pos, key_pos, scale):
    scores = masked_scores(queries, keys, query_pos, key_pos, scale)
    shares = jnp.exp(scores - logsum[..., None])
    share_grad = jnp.einsum("cgd,ld->gcl", context_grad, values, preferred_element_type=jnp.float32)
    share_dot = jnp.sum(shares * share_grad, axis=-1, keepdims=True)
    score_low = (shares * (share_grad - share_dot)).astype(jnp.bfloat16)
    query_part = (
        jnp.einsum("gcl,ld->cgd", score_low, keys, preferred_element_type=jnp.float32) * scale
    )
    key_part = (
        jnp.einsum("gcl,cgd->ld", score_low, queries, preferred_element_type=jnp.float32) * scale
    )
    value_part = jnp.einsum(
        "gcl,cgd->ld",
        shares.astype(jnp.bfloat16),
        context_grad,
        preferred_element_type=jnp.float32,
    )
    return (query_part, key_part, value_part)


def body(
    hidden_in,
    cotangent,
    block_order,
    query_weight,
    keyval_weight,
    output_weight,
    gate_weight,
    up_weight,
    down_weight,
    attn_gain,
    ffn_gain,
    query_gain,
    key_gain,
):
    sequences, _, own_rows, width = hidden_in.shape
    tensor_size = lax.axis_size("tensor")
    heads_size = lax.axis_size("heads")
    chips = heads_size // 2
    shard_rows = own_rows * heads_size
    block_len = shard_rows // 2
    seq_len = shard_rows * tensor_size
    head_dim = query_gain.shape[0]
    units = gate_weight.shape[1]
    query_width = query_weight.shape[2]
    group_size = query_width // head_dim
    scale = head_dim ** (-0.5)
    rank = lax.axis_index("tensor")
    head_rank = lax.axis_index("heads")
    hidden_own = hidden_in[:, 0]
    cot_own = cotangent[:, 0]

    chip_at = lax.rem(head_rank // 2 - jnp.arange(chips, dtype=jnp.int32) + chips, chips)
    core_at = lax.rem(head_rank + jnp.arange(2, dtype=jnp.int32), 2)
    head_at = (chip_at[:, None] * 2 + core_at[None, :]).reshape(heads_size)
    row_at = (head_at[:, None] * own_rows + jnp.arange(own_rows, dtype=jnp.int32)[None, :]).reshape(
        shard_rows
    )
    rank_at = lax.rem(rank - jnp.arange(tensor_size, dtype=jnp.int32) + tensor_size, tensor_size)
    order_at = block_order[rank_at]
    second = row_at >= block_len
    key_pos = (
        jnp.where(second[None, :], order_at[:, 1:2], order_at[:, 0:1]) * block_len
        + lax.rem(row_at, block_len)[None, :]
    )
    query_pos = key_pos[0]
    key_pos = key_pos.reshape(seq_len)
    cosine, sine = rope_tables(query_pos, head_dim)
    cos_query = cosine[None, :, None, :]
    sin_query = sine[None, :, None, :]
    cos_key = cosine[None]
    sin_key = sine[None]

    attn_own = jnp.concatenate(
        [query_weight[:, 0], keyval_weight[:, 0], output_weight[:, 0]], axis=1
    )
    attn_all = lax.all_gather(attn_own, ("fsdp", "tensor"), axis=0, tiled=True)
    feed_own = jnp.concatenate([gate_weight, up_weight, down_weight], axis=1)
    feed_all = lax.all_gather(feed_own, ("fsdp", "heads"), axis=0, tiled=True)
    qkv_all = attn_all[:, : 2 * query_width]
    output_all = attn_all[:, 2 * query_width :]
    gate_up_all = feed_all[:, : 2 * units]
    down_all = feed_all[:, 2 * units :]

    def to_sequence(values):
        values = values.reshape(2, chips, sequences, own_rows, values.shape[-1])
        return values.transpose(2, 1, 0, 3, 4).reshape(sequences, shard_rows, values.shape[-1])

    def from_sequence(values):
        values = values.reshape(sequences, chips, 2, own_rows, values.shape[-1])
        return values.transpose(2, 1, 0, 3, 4).reshape(sequences * shard_rows, values.shape[-1])

    inputs = hidden_own.astype(jnp.float32)
    scale_one = rms_scale(inputs)
    normed_one = (inputs * scale_one * attn_gain).astype(jnp.bfloat16)
    rows_flat = gather_heads(normed_one).reshape(sequences * shard_rows, width)
    cot_flat = jnp.stack(gather_ring(cot_own, "tensor")).reshape(-1, width)
    qkv_raw = to_sequence(matmul(rows_flat, qkv_all))
    query_raw = qkv_raw[..., :query_width].reshape(sequences, shard_rows, group_size, head_dim)
    key_raw = qkv_raw[..., query_width : query_width + head_dim]
    value_raw = qkv_raw[..., query_width + head_dim :]
    query_scale = rms_scale(query_raw)
    key_scale = rms_scale(key_raw)
    query_rot = rotate(query_raw * query_scale * query_gain, cos_query, sin_query).astype(
        jnp.bfloat16
    )
    key_rot = rotate(key_raw * key_scale * key_gain, cos_key, sin_key).astype(jnp.bfloat16)
    sending = jnp.concatenate([key_rot, value_raw.astype(jnp.bfloat16)], axis=-1)
    gathered = jnp.stack(gather_ring(sending, "tensor"), axis=1)
    gathered = gathered.reshape(sequences, seq_len, 2 * head_dim)
    keys_all = gathered[..., :head_dim]
    values_all = gathered[..., head_dim:]

    halves = [slice(0, block_len), slice(block_len, shard_rows)]
    contexts = []
    logsums = []
    for seq in range(sequences):
        pieces = [
            attend(
                query_rot[seq, half], keys_all[seq], values_all[seq], query_pos[half], key_pos, scale
            )
            for half in halves
        ]
        contexts.append(jnp.concatenate([piece[0] for piece in pieces]))
        logsums.append([piece[1] for piece in pieces])
    context_flat = from_sequence(
        jnp.stack(contexts).reshape(sequences, shard_rows, query_width)
    )
    branch_part = contract_cols(context_flat, output_all).astype(jnp.bfloat16)
    branch = scatter_heads(branch_part.reshape(2, chips, sequences, own_rows, width))
    middle = inputs + branch
    scale_two = rms_scale(middle)
    normed_two = (middle * scale_two * ffn_gain).astype(jnp.bfloat16)
    two_flat = jnp.stack(gather_ring(normed_two, "tensor")).reshape(-1, width)
    gate_up = matmul(two_flat, gate_up_all)
    gate_value = gate_up[:, :units]
    upper_value = gate_up[:, units:]
    sigmoid_gate = jax.nn.sigmoid(gate_value)
    activated = gate_value * sigmoid_gate
    hidden = (activated * upper_value).astype(jnp.bfloat16)
    hidden_grad = matmul(cot_flat, down_all)
    gate_low = (
        hidden_grad * upper_value * sigmoid_gate * (1.0 + gate_value * (1.0 - sigmoid_gate))
    ).astype(jnp.bfloat16)
    upper_low = (hidden_grad * activated).astype(jnp.bfloat16)
    both_low = jnp.concatenate([gate_low, upper_low], axis=1)
    normed_two_part = contract_cols(both_low, gate_up_all).reshape(
        tensor_size, sequences, own_rows, width
    )
    normed_two_grad = scatter_tensor(normed_two_part.astype(jnp.bfloat16), normed_two_part[0])
    middle_norm_grad, ffn_terms = norm_back(middle, scale_two, ffn_gain, normed_two_grad)
    middle_grad = cot_own.astype(jnp.float32) + middle_norm_grad
    branch_low = middle_grad.astype(jnp.bfloat16)
    feed_part = contract_cols(hidden, down_all).reshape(tensor_size, sequences, own_rows, width)
    feed = scatter_tensor(feed_part.astype(jnp.bfloat16), feed_part[0])
    block_out = (middle + feed).astype(jnp.bfloat16)
    feed_grad = jnp.concatenate(
        [
            contract_rows(two_flat, both_low).astype(jnp.bfloat16),
            contract_rows(cot_flat, hidden).astype(jnp.bfloat16),
        ],
        axis=1,
    )
    feed_grad = lax.psum_scatter(
        feed_grad, ("fsdp", "heads"), scatter_dimension=0, tiled=True
    ).astype(jnp.float32)

    branch_flat = gather_heads(branch_low).reshape(sequences * shard_rows, width)
    context_grad = to_sequence(matmul(branch_flat, output_all).astype(jnp.bfloat16))
    context_grad = context_grad.reshape(sequences, shard_rows, group_size, head_dim)
    output_grad = contract_rows(branch_flat, context_flat)

    query_parts = []
    key_totals = []
    for seq in range(sequences):
        pieces = [
            attend_back(
                query_rot[seq, half],
                keys_all[seq],
                values_all[seq],
                logsums[seq][at],
                context_grad[seq, half],
                query_pos[half],
                key_pos,
                scale,
            )
            for at, half in enumerate(halves)
        ]
        query_parts.append(jnp.concatenate([piece[0] for piece in pieces]))
        key_totals.append(
            jnp.concatenate(
                [pieces[0][1] + pieces[1][1], pieces[0][2] + pieces[1][2]], axis=-1
            ).reshape(tensor_size, shard_rows, 2 * head_dim)
        )
    kv_terms = jnp.stack(key_totals, axis=1)
    kv_own = scatter_tensor(kv_terms.astype(jnp.bfloat16), kv_terms[0])
    key_rot_grad = kv_own[..., :head_dim]
    value_grad = kv_own[..., head_dim:]
    query_rot_grad = jnp.stack(query_parts)
    query_norm_grad = rotate_back(query_rot_grad, cos_query, sin_query)
    query_raw_grad, query_terms = norm_back(query_raw, query_scale, query_gain, query_norm_grad)
    key_norm_grad = rotate_back(key_rot_grad, cos_key, sin_key)
    key_raw_grad, key_terms = norm_back(key_raw, key_scale, key_gain, key_norm_grad)
    qkv_low = from_sequence(
        jnp.concatenate(
            [
                query_raw_grad.reshape(sequences, shard_rows, query_width),
                key_raw_grad,
                value_grad,
            ],
            axis=-1,
        ).astype(jnp.bfloat16)
    )
    normed_one_part = contract_cols(qkv_low, qkv_all).astype(jnp.bfloat16)
    normed_one_grad = scatter_heads(
        normed_one_part.reshape(2, chips, sequences, own_rows, width)
    )
    qkv_grad = contract_rows(rows_flat, qkv_low)
    attn_grad = jnp.concatenate([qkv_grad, output_grad], axis=1)
    attn_grad = scatter_rows(scatter_rows(attn_grad, "fsdp"), "tensor")
    attn_gain_part = jnp.sum(qkv_grad * qkv_all.astype(jnp.float32), axis=1) / attn_gain
    gains = reduce_all(
        jnp.concatenate(
            [
                attn_gain_part,
                jnp.sum(ffn_terms, axis=(0, 1)),
                jnp.sum(query_terms, axis=(0, 1, 2)),
                jnp.sum(key_terms, axis=(0, 1)),
            ]
        )
    )
    input_norm_grad, _ = norm_back(inputs, scale_one, attn_gain, normed_one_grad)
    input_grad = middle_grad + input_norm_grad
    return (
        block_out[:, None],
        input_grad[:, None],
        attn_grad[:, None, :query_width],
        attn_grad[:, None, query_width : 2 * query_width],
        attn_grad[:, None, 2 * query_width :],
        feed_grad[:, :units],
        feed_grad[:, units : 2 * units],
        feed_grad[:, 2 * units :],
        gains[:width],
        gains[width : 2 * width],
        gains[2 * width : 2 * width + head_dim],
        gains[2 * width + head_dim :],
    )


def solution(mesh):
    placed = (
        P("fsdp", "tensor", "heads", None),
        P("fsdp", "tensor", "heads", None),
        P(),
        P(("fsdp", "tensor"), "heads", None),
        P(("fsdp", "tensor"), "heads", None),
        P(("fsdp", "tensor"), "heads", None),
        P(("fsdp", "heads"), "tensor"),
        P(("fsdp", "heads"), "tensor"),
        P(("fsdp", "heads"), "tensor"),
        P(),
        P(),
        P(),
        P(),
    )
    return jax.shard_map(
        body,
        mesh=mesh,
        in_specs=placed,
        out_specs=(
            P("fsdp", "tensor", "heads", None),
            P("fsdp", "tensor", "heads", None),
            P(("fsdp", "tensor"), "heads", None),
            P(("fsdp", "tensor"), "heads", None),
            P(("fsdp", "tensor"), "heads", None),
            P(("fsdp", "heads"), "tensor"),
            P(("fsdp", "heads"), "tensor"),
            P(("fsdp", "heads"), "tensor"),
            P(),
            P(),
            P(),
            P(),
        ),
        check_vma=False,
    )
```

time: 1060 us -> 372 us (0.35)
  waiting for transfers between devices: 748 us -> 98.4 us
  blocking collectives: 132 us -> 25.1 us
  starting transfers between devices: 1.78 us -> 56.3 us
  other arithmetic: 37.3 us -> 56.6 us
    reduce_scatter x10 -> x1, waiting for transfers between devices: 480 us -> 0.01 us  [body(): lax.psum_scatter(feed_grad, ('fsdp', 'heads'), scatter_dimension=0, tiled...]
    all_gather x8 -> x1, waiting for transfers between devices: 203 us -> 0.01 us  [body(): feed_all = lax.all_gather(feed_own, ('fsdp', 'heads'), axis=0, tiled=True)]
    ppermute x0 -> x50, waiting for transfers between devices: none -> 98.4 us  [the longest x30 60.5 us: shift_chips(): lax.ppermute(values, axis, [(i, (i + step) % size) for i in range(size)])]
    unnamed x20 -> x2, waiting for transfers between devices: 64.9 us -> 0.03 us
    psum x1 -> x0, blocking collectives: 63 us -> none  [body(): lax.psum((jnp.sum(attn_terms, axis=(0, 1, 2)), jnp.sum(ffn_terms, axis=(0...]
    ppermute x0 -> x50, starting transfers between devices: none -> 56.2 us  [the longest x30 38.4 us: shift_chips(): lax.ppermute(values, axis, [(i, (i + step) % size) for i in range(size)])]
    all_gather x3 -> x1, blocking collectives: 68.8 us -> 25.1 us  [body(): attn_all = lax.all_gather(attn_own, ('fsdp', 'tensor'), axis=0, tiled=True)]
    dot_general x28 -> x24, matrix products: 23.1 us -> 40.9 us  [the longest x4 13.3 us: attend_back(): jnp.einsum('cgd,ld->gcl', context_grad, values, preferred_element_type=jn...]
  transfers between devices with their start and end apart: 19 -> 52, of which waited for: 16 -> 31; matrix products, arithmetic and copies ran while one was open for 7% -> 40% of each run, Pallas kernels for 0% -> 0%
where the time goes in v1:
time: 372 us; the launch traced here: 366 us
  waiting for transfers between devices  98.4 us (26%)
  matrix products  69 us (19%)
  other arithmetic  56.6 us (15%)
  starting transfers between devices  56.3 us (15%)
  local copies, waits for them, and re-layouts  45 us (12%)
  blocking collectives  25.1 us (7%)
  between operations  15.8 us (4%)
    ppermute x30, waiting for transfers between devices, shift_chips(): lax.ppermute(values, axis, [(i, (i + step) % size) for i in range(size)])  60.5 us
    ppermute x30, starting transfers between devices, shift_chips(): lax.ppermute(values, axis, [(i, (i + step) % size) for i in range(size)])  38.4 us
    ppermute x15, waiting for transfers between devices, shift_z(): lax.ppermute(values, 'heads', [(i, (i + 2 * step) % size) for i in range(...  37.8 us
    all_gather x1, blocking collectives, body(): attn_all = lax.all_gather(attn_own, ('fsdp', 'tensor'), axis=0, tiled=True)  25.1 us
    ppermute x15, starting transfers between devices, shift_z(): lax.ppermute(values, 'heads', [(i, (i + 2 * step) % size) for i in range(...  17.7 us
    dot_general x4, matrix products, attend_back(): jnp.einsum('cgd,ld->gcl', context_grad, values, preferred_element_type=jn...  13.3 us
    unnamed x183, local copies, waits for them, and re-layouts  12.6 us
    dot_general x4, matrix products, contract_rows(): lax.dot_general(left, right, (((0,), (0,)), ((), ())), preferred_element_...  11.3 us
  transfers between devices with their start and end apart: 52, of which 31 were waited for; matrix products, arithmetic and copies ran while one was open for 40% of the time, Pallas kernels for 0%

profile of v1, /device:TPU:24, one launch (start us, length us, event | category | flops | bytes accessed | tf_op | source)
XLA Modules:
  0.0 366.3 jit_solution(399703757464927754)
XLA Ops:
  9.4 4.1 %collective-permute-start.2 = (bf16[2,64,1024]{2,1,0:T(8,128)(2,1)S(1)}, bf16[2,64,1024]{2,1,0:T(8,128)(2,1)S(1)}, u32[]{:S(2)}, u32[]{:S(2)}) collective-permute-start(bf16[2,64,1024]{2,1,0:T(8,128)(2,1)S(1)} %fusion.66), channel_id=1, source_target_pairs={{0,24},{4,28},{8,0},{12,4},{16,8},{20,12},{24,16},{28,20},{1,25},{... | collective-permute-start | bytes 786440 | tf_op jit(solution)/shard_map/ppermute | solution.py:73
  19.6 5.1 %collective-permute-done.2 = bf16[2,64,1024]{2,1,0:T(8,128)(2,1)S(1)} collective-permute-done((bf16[2,64,1024]{2,1,0:T(8,128)(2,1)S(1)}, bf16[2,64,1024]{2,1,0:T(8,128)(2,1)S(1)}, u32[]{:S(2)}, u32[]{:S(2)}) %collective-permute-start.2) | collective-permute-done | bytes 262176 | tf_op jit(solution)/shard_map/ppermute | solution.py:73
  30.0 25.1 %all_gather.6 = bf16[1024,384]{1,0:T(8,128)(2,1)S(1)} all-gather(bf16[64,384]{1,0:T(8,128)(2,1)S(1)} %pad_maximum_fusion.26), channel_id=1, replica_groups=mesh['fsdp'=4,'heads'=8,'tensor'=4] {'fsdp','tensor'}, dimensions={0}, use_global_device_ids=true | all-gather | bytes 835584 | tf_op jit(solution)/shard_map/all_gather | solution.py:220
  66.2 5.0 %collective-permute-done.6 = bf16[2,512,128]{2,1,0:T(8,128)(2,1)S(1)} collective-permute-done((bf16[2,512,128]{2,1,0:T(8,128)(2,1)}, bf16[2,512,128]{2,1,0:T(8,128)(2,1)S(1)}, u32[]{:S(2)}, u32[]{:S(2)}) %collective-permute-start.6) | collective-permute-done | bytes 262176 | tf_op jit(solution)/shard_map/ppermute | solution.py:68
  102.3 4.9 %collective-permute-done.18 = bf16[2,64,1024]{2,1,0:T(8,128)(2,1)S(1)} collective-permute-done((bf16[2,64,1024]{2,1,0:T(8,128)(2,1)S(1)}, bf16[2,64,1024]{2,1,0:T(8,128)(2,1)S(1)}, u32[]{:S(2)}, u32[]{:S(2)}) %collective-permute-start.18) | collective-permute-done | bytes 262176 | tf_op jit(solution)/shard_map/ppermute | solution.py:68
  107.2 5.2 %collective-permute-done.17 = bf16[2,64,1024]{2,1,0:T(8,128)(2,1)S(1)} collective-permute-done((bf16[2,64,1024]{2,1,0:T(8,128)(2,1)S(1)}, bf16[2,64,1024]{2,1,0:T(8,128)(2,1)S(1)}, u32[]{:S(2)}, u32[]{:S(2)}) %collective-permute-start.17) | collective-permute-done | bytes 262176 | tf_op jit(solution)/shard_map/ppermute | solution.py:68
  124.0 4.3 %collective-permute-done.8 = bf16[2,64,1024]{2,1,0:T(8,128)(2,1)S(1)} collective-permute-done((bf16[2,64,1024]{2,1,0:T(8,128)(2,1)S(1)}, bf16[2,64,1024]{2,1,0:T(8,128)(2,1)S(1)}, u32[]{:S(2)}, u32[]{:S(2)}) %collective-permute-start.8) | collective-permute-done | bytes 262176 | tf_op jit(solution)/shard_map/ppermute | solution.py:73
  128.3 4.6 %collective-permute-done.10 = bf16[2,64,1024]{2,1,0:T(8,128)(2,1)S(1)} collective-permute-done((bf16[2,64,1024]{2,1,0:T(8,128)(2,1)S(1)}, bf16[2,64,1024]{2,1,0:T(8,128)(2,1)S(1)}, u32[]{:S(2)}, u32[]{:S(2)}) %collective-permute-start.10) | collective-permute-done | bytes 262176 | tf_op jit(solution)/shard_map/ppermute | solution.py:73
  137.8 6.3 %collective-permute-done.12 = bf16[2,64,1024]{2,1,0:T(8,128)(2,1)S(1)} collective-permute-done((bf16[2,64,1024]{2,1,0:T(8,128)(2,1)S(1)}, bf16[2,64,1024]{2,1,0:T(8,128)(2,1)S(1)}, u32[]{:S(2)}, u32[]{:S(2)}) %collective-permute-start.12) | collective-permute-done | bytes 262176 | tf_op jit(solution)/shard_map/ppermute | solution.py:68
  144.1 4.7 %collective-permute-done.11 = bf16[2,64,1024]{2,1,0:T(8,128)(2,1)S(1)} collective-permute-done((bf16[2,64,1024]{2,1,0:T(8,128)(2,1)S(1)}, bf16[2,64,1024]{2,1,0:T(8,128)(2,1)S(1)}, u32[]{:S(2)}, u32[]{:S(2)}) %collective-permute-start.11) | collective-permute-done | bytes 262176 | tf_op jit(solution)/shard_map/ppermute | solution.py:68
  149.9 5.4 %fusion.14 = f32[512,2304]{1,0:T(8,128)S(1)} fusion(bf16[512,1024]{1,0:T(8,128)(2,1)} %bitcast.449, bf16[1024,3456]{1,0:T(8,128)(2,1)} %all-gather.2.cloned.1.call-done), kind=kOutput, calls=%fused_computation.41 | convolution fusion | flops 2415919104 | bytes 10485760 | tf_op jit(solution)/shard_map/dot_general | solution.py:47
  164.1 4.3 %convolution_convert_fusion = bf16[1024,2304]{1,0:T(8,128)(2,1)} fusion(bf16[512,1024]{1,0:T(8,128)(2,1)S(1)} %bitcast.450, bf16[512,1152]{1,0:T(8,128)(2,1)S(1)} %get-tuple-element.58, bf16[512,1152]{1,0:T(8,128)(2,1)S(1)} %get-tuple-element.57), kind=kOutput, calls=%fused_computation.2 | convolution fusion | flops 2422996992 | bytes 8126464 | tf_op jit(solution)/shard_map/dot_general | solution.py:51
  168.4 5.9 %collective-permute-done.22 = bf16[2,64,1024]{2,1,0:T(8,128)(2,1)S(1)} collective-permute-done((bf16[2,64,1024]{2,1,0:T(8,128)(2,1)S(1)}, bf16[2,64,1024]{2,1,0:T(8,128)(2,1)S(1)}, u32[]{:S(2)}, u32[]{:S(2)}) %collective-permute-start.22) | collective-permute-done | bytes 262176 | tf_op jit(solution)/shard_map/ppermute | solution.py:68
  182.7 5.5 %collective-permute-done.25 = bf16[2,64,1024]{2,1,0:T(8,128)(2,1)S(1)} collective-permute-done((bf16[2,64,1024]{2,1,0:T(8,128)(2,1)S(1)}, bf16[2,64,1024]{2,1,0:T(8,128)(2,1)S(1)}, u32[]{:S(2)}, u32[]{:S(2)}) %collective-permute-start.25) | collective-permute-done | bytes 262176 | tf_op jit(solution)/shard_map/ppermute | solution.py:73
  190.7 4.3 %collective-permute-done.23 = bf16[2,64,1024]{2,1,0:T(8,128)(2,1)S(1)} collective-permute-done((bf16[2,64,1024]{2,1,0:T(8,128)(2,1)S(1)}, bf16[2,64,1024]{2,1,0:T(8,128)(2,1)S(1)}, u32[]{:S(2)}, u32[]{:S(2)}) %collective-permute-start.23) | collective-permute-done | bytes 262176 | tf_op jit(solution)/shard_map/ppermute | solution.py:73
  201.3 6.5 %pad_maximum_fusion = bf16[1024,3456]{1,0:T(8,128)(2,1)} fusion(bf16[1024,1152]{1,0:T(8,128)(2,1)} %convolution_convert_fusion.1, bf16[1024,2304]{1,0:T(8,128)(2,1)} %convolution_convert_fusion), kind=kLoop, calls=%fused_computation.1 | loop fusion | flops 14155776 | bytes 14155776 | tf_op jit(solution)/shard_map/concatenate | solution.py:300
  217.3 4.1 %fusion.3 = (f32[2,256]{1,0:T(2,128)}, f32[2048,256,2]{1,0,2:T(8,128)}) fusion(f32[2,256,2048]{1,2,0:T(8,128)S(1)} %copy-done.7, f32[2,256]{1,0:T(2,128)} %log_add_fusion.1, bf16[1,256,2,64]{1,3,2,0:T(8,128)(2,1)S(1)} %copy.191, bf16[2,2048,128]{1,2,0:T(8,128)(2,1)S(1)} %reshape.544), kind=kOutput, calls=%fused_computation.10 | convolution fusion | flops 137362944 | bytes 8720384 | tf_op jit(solution)/shard_map/cgd,ld->gcl/dot_general | solution.py:146
  221.5 4.1 %convolution_bitcast_fusion.5 = f32[2048,64]{0,1:T(8,128)} fusion(f32[2,256,2048]{1,2,0:T(8,128)} %copy-done.2, f32[2,256]{1,0:T(2,128)S(1)} %copy-done.62, bf16[1,256,2,64]{1,3,2,0:T(8,128)(2,1)S(1)} %copy.189), kind=kOutput, calls=%fused_computation.74 | convolution fusion | flops 136314880 | bytes 4786176 | tf_op jit(solution)/shard_map/gcl,cgd->ld/dot_general | solution.py:155
  245.0 4.4 %fusion.11 = bf16[2,256,2048]{1,2,0:T(8,128)(2,1)S(1)} fusion(f32[2048,256,2]{1,0,2:T(8,128)} %get-tuple-element.140, f32[2,256,2048]{1,2,0:T(8,128)} %copy-done.2, f32[2,256]{1,0:T(2,128)} %get-tuple-element.139, f32[2,256]{1,0:T(2,128)} %log_add_fusion.3), kind=kLoop, calls=%fused_computation.22 | loop fusion | flops 4194304 | bytes 10489856 | tf_op jit(solution)/shard_map/convert_element_type | solution.py:148
  272.9 4.3 %collective-permute-start.29 = (bf16[2,512,128]{2,1,0:T(8,128)(2,1)}, bf16[2,512,128]{2,1,0:T(8,128)(2,1)}, u32[]{:S(2)}, u32[]{:S(2)}) collective-permute-start(bf16[2,512,128]{2,1,0:T(8,128)(2,1)} %get-tuple-element.79), channel_id=1, source_target_pairs={{0,1},{1,2},{2,3},{3,0},{4,5},{5,6},{6,7},{7,4},{8,9},{9,10},{10,1... | collective-permute-start | bytes 786440 | tf_op jit(solution)/shard_map/ppermute | solution.py:68
  278.3 5.1 %collective-permute-done.27 = bf16[2,512,128]{2,1,0:T(8,128)(2,1)} collective-permute-done((bf16[2,512,128]{2,1,0:T(8,128)(2,1)}, bf16[2,512,128]{2,1,0:T(8,128)(2,1)}, u32[]{:S(2)}, u32[]{:S(2)}) %collective-permute-start.27) | collective-permute-done | bytes 262176 | tf_op jit(solution)/shard_map/ppermute | solution.py:68
  283.5 3.8 %collective-permute-done.29 = bf16[2,512,128]{2,1,0:T(8,128)(2,1)} collective-permute-done((bf16[2,512,128]{2,1,0:T(8,128)(2,1)}, bf16[2,512,128]{2,1,0:T(8,128)(2,1)}, u32[]{:S(2)}, u32[]{:S(2)}) %collective-permute-start.29) | collective-permute-done | bytes 262176 | tf_op jit(solution)/shard_map/ppermute | solution.py:68
  312.7 3.7 %collective-permute-done.44 = f32[2176]{0:T(1024)S(1)} collective-permute-done((f32[2176]{0:T(1024)S(1)}, f32[2176]{0:T(1024)S(1)}, u32[]{:S(2)}, u32[]{:S(2)}) %collective-permute-start.44) | collective-permute-done | bytes 8736 | tf_op jit(solution)/shard_map/ppermute | solution.py:68
  350.9 3.7 %collective-permute-done.15 = bf16[2,64,1024]{2,1,0:T(8,128)(2,1)S(1)} collective-permute-done((bf16[2,64,1024]{2,1,0:T(8,128)(2,1)}, bf16[2,64,1024]{2,1,0:T(8,128)(2,1)S(1)}, u32[]{:S(2)}, u32[]{:S(2)}) %collective-permute-start.15) | collective-permute-done | bytes 262176 | tf_op jit(solution)/shard_map/ppermute | solution.py:68
  (437 shorter events, 216.1 us)
Async XLA Ops:
  7.2 142.7 %all-gather.2.cloned.1.call-start = ((), (), s32[]{:S(2)}) async-start(), calls=%async_computation.1 | async-start | bytes 7299072 | tf_op jit(solution)/shard_map/all_gather | solution.py:222
  9.4 15.3 %collective-permute-start.2 = (bf16[2,64,1024]{2,1,0:T(8,128)(2,1)S(1)}, bf16[2,64,1024]{2,1,0:T(8,128)(2,1)S(1)}, u32[]{:S(2)}, u32[]{:S(2)}) collective-permute-start(bf16[2,64,1024]{2,1,0:T(8,128)(2,1)S(1)} %fusion.66), channel_id=1, source_target_pairs={{0,24},{4,28},{8,0},{12,4},{16,8},{20,12},{24,16},{28,20},{1,25},{... | collective-permute-start | bytes 786440 | tf_op jit(solution)/shard_map/ppermute | solution.py:73
  13.6 11.2 %collective-permute-start.1 = (bf16[2,64,1024]{2,1,0:T(8,128)(2,1)S(1)}, bf16[2,64,1024]{2,1,0:T(8,128)(2,1)S(1)}, u32[]{:S(2)}, u32[]{:S(2)}) collective-permute-start(bf16[2,64,1024]{2,1,0:T(8,128)(2,1)S(1)} %fusion.66), channel_id=1, source_target_pairs={{0,16},{4,20},{8,24},{12,28},{16,0},{20,4},{24,8},{28,12},{1,17},{... | collective-permute-start | bytes 786440 | tf_op jit(solution)/shard_map/ppermute | solution.py:73
  13.6 14.6 %collective-permute-start = (bf16[2,64,1024]{2,1,0:T(8,128)(2,1)S(1)}, bf16[2,64,1024]{2,1,0:T(8,128)(2,1)S(1)}, u32[]{:S(2)}, u32[]{:S(2)}) collective-permute-start(bf16[2,64,1024]{2,1,0:T(8,128)(2,1)S(1)} %fusion.66), channel_id=1, source_target_pairs={{0,8},{4,12},{8,16},{12,20},{16,24},{20,28},{24,0},{28,4},{1,9},{5... | collective-permute-start | bytes 786440 | tf_op jit(solution)/shard_map/ppermute | solution.py:73
  16.5 341.0 %reduce-scatter.2.cloned.1.call-start = ((), (), s32[]{:S(2)}) async-start(), calls=%async_computation.2 | async-start | bytes 7299072 | tf_op jit(solution)/shard_map/reduce_scatter | solution.py:307
  29.3 27.3 %collective-permute-start.3 = (bf16[4,2,64,1024]{3,2,1,0:T(8,128)(2,1)}, bf16[4,2,64,1024]{3,2,1,0:T(8,128)(2,1)}, u32[]{:S(2)}, u32[]{:S(2)}) collective-permute-start(bf16[4,2,64,1024]{3,2,1,0:T(8,128)(2,1)} %get-tuple-element.95), channel_id=1, source_target_pairs={{0,4},{4,0},{8,12},{12,8},{16,20},{20,16},{24,28},{28,24},{1,5},{5... | collective-permute-start | bytes 3145736 | tf_op jit(solution)/shard_map/ppermute | solution.py:78
  96.6 18.8 %collective-permute-start.7 = (bf16[4,2,64,1024]{3,2,1,0:T(8,128)(2,1)}, bf16[4,2,64,1024]{3,2,1,0:T(8,128)(2,1)}, u32[]{:S(2)}, u32[]{:S(2)}) collective-permute-start(bf16[4,2,64,1024]{3,2,1,0:T(8,128)(2,1)} %bitcast.47), channel_id=1, source_target_pairs={{0,4},{4,0},{8,12},{12,8},{16,20},{20,16},{24,28},{28,24},{1,5},{5... | collective-permute-start | bytes 3145736 | tf_op jit(solution)/shard_map/ppermute | solution.py:78
  98.4 14.0 %collective-permute-start.17 = (bf16[2,64,1024]{2,1,0:T(8,128)(2,1)S(1)}, bf16[2,64,1024]{2,1,0:T(8,128)(2,1)S(1)}, u32[]{:S(2)}, u32[]{:S(2)}) collective-permute-start(bf16[2,64,1024]{2,1,0:T(8,128)(2,1)S(1)} %bitcast.433), channel_id=1, source_target_pairs={{0,1},{1,2},{2,3},{3,0},{4,5},{5,6},{6,7},{7,4},{8,9},{9,10},{10,1... | collective-permute-start | bytes 786440 | tf_op jit(solution)/shard_map/ppermute | solution.py:68
  100.4 12.0 %collective-permute-start.19 = (bf16[2,64,1024]{2,1,0:T(8,128)(2,1)S(1)}, bf16[2,64,1024]{2,1,0:T(8,128)(2,1)S(1)}, u32[]{:S(2)}, u32[]{:S(2)}) collective-permute-start(bf16[2,64,1024]{2,1,0:T(8,128)(2,1)S(1)} %bitcast.434), channel_id=1, source_target_pairs={{0,3},{1,0},{2,1},{3,2},{4,7},{5,4},{6,5},{7,6},{8,11},{9,8},{10,9... | collective-permute-start | bytes 786440 | tf_op jit(solution)/shard_map/ppermute | solution.py:68
  118.2 14.7 %collective-permute-start.10 = (bf16[2,64,1024]{2,1,0:T(8,128)(2,1)S(1)}, bf16[2,64,1024]{2,1,0:T(8,128)(2,1)S(1)}, u32[]{:S(2)}, u32[]{:S(2)}) collective-permute-start(bf16[2,64,1024]{2,1,0:T(8,128)(2,1)S(1)} %get-tuple-element.90), channel_id=1, source_target_pairs={{0,8},{4,12},{8,16},{12,20},{16,24},{20,28},{24,0},{28,4},{1,9},{5... | collective-permute-start | bytes 786440 | tf_op jit(solution)/shard_map/ppermute | solution.py:73
  119.2 13.7 %collective-permute-start.9 = (bf16[2,64,1024]{2,1,0:T(8,128)(2,1)S(1)}, bf16[2,64,1024]{2,1,0:T(8,128)(2,1)S(1)}, u32[]{:S(2)}, u32[]{:S(2)}) collective-permute-start(bf16[2,64,1024]{2,1,0:T(8,128)(2,1)S(1)} %get-tuple-element.91), channel_id=1, source_target_pairs={{0,24},{4,28},{8,0},{12,4},{16,8},{20,12},{24,16},{28,20},{1,25},{... | collective-permute-start | bytes 786440 | tf_op jit(solution)/shard_map/ppermute | solution.py:73
  135.0 13.8 %collective-permute-start.11 = (bf16[2,64,1024]{2,1,0:T(8,128)(2,1)S(1)}, bf16[2,64,1024]{2,1,0:T(8,128)(2,1)S(1)}, u32[]{:S(2)}, u32[]{:S(2)}) collective-permute-start(bf16[2,64,1024]{2,1,0:T(8,128)(2,1)S(1)} %multiply_convert_fusion.4), channel_id=1, source_target_pairs={{0,1},{1,2},{2,3},{3,0},{4,5},{5,6},{6,7},{7,4},{8,9},{9,10},{10,1... | collective-permute-start | bytes 786440 | tf_op jit(solution)/shard_map/ppermute | solution.py:68
  137.1 11.7 %collective-permute-start.13 = (bf16[2,64,1024]{2,1,0:T(8,128)(2,1)S(1)}, bf16[2,64,1024]{2,1,0:T(8,128)(2,1)S(1)}, u32[]{:S(2)}, u32[]{:S(2)}) collective-permute-start(bf16[2,64,1024]{2,1,0:T(8,128)(2,1)S(1)} %multiply_convert_fusion.4), channel_id=1, source_target_pairs={{0,3},{1,0},{2,1},{3,2},{4,7},{5,4},{6,5},{7,6},{8,11},{9,8},{10,9... | collective-permute-start | bytes 786440 | tf_op jit(solution)/shard_map/ppermute | solution.py:68
  160.2 14.1 %collective-permute-start.22 = (bf16[2,64,1024]{2,1,0:T(8,128)(2,1)S(1)}, bf16[2,64,1024]{2,1,0:T(8,128)(2,1)S(1)}, u32[]{:S(2)}, u32[]{:S(2)}) collective-permute-start(bf16[2,64,1024]{2,1,0:T(8,128)(2,1)S(1)} %bitcast.464), channel_id=1, source_target_pairs={{0,1},{1,2},{2,3},{3,0},{4,5},{5,6},{6,7},{7,4},{8,9},{9,10},{10,1... | collective-permute-start | bytes 786440 | tf_op jit(solution)/shard_map/ppermute | solution.py:68
  162.9 11.4 %collective-permute-start.20 = (bf16[2,64,1024]{2,1,0:T(8,128)(2,1)S(1)}, bf16[2,64,1024]{2,1,0:T(8,128)(2,1)S(1)}, u32[]{:S(2)}, u32[]{:S(2)}) collective-permute-start(bf16[2,64,1024]{2,1,0:T(8,128)(2,1)S(1)} %bitcast.463), channel_id=1, source_target_pairs={{0,2},{1,3},{2,0},{3,1},{4,6},{5,7},{6,4},{7,5},{8,10},{9,11},{10,... | collective-permute-start | bytes 786440 | tf_op jit(solution)/shard_map/ppermute | solution.py:68
  163.2 14.7 %collective-permute-start.21 = (bf16[2,64,1024]{2,1,0:T(8,128)(2,1)S(1)}, bf16[2,64,1024]{2,1,0:T(8,128)(2,1)S(1)}, u32[]{:S(2)}, u32[]{:S(2)}) collective-permute-start(bf16[2,64,1024]{2,1,0:T(8,128)(2,1)S(1)} %bitcast.462), channel_id=1, source_target_pairs={{0,3},{1,0},{2,1},{3,2},{4,7},{5,4},{6,5},{7,6},{8,11},{9,8},{10,9... | collective-permute-start | bytes 786440 | tf_op jit(solution)/shard_map/ppermute | solution.py:68
  180.3 14.7 %collective-permute-start.23 = (bf16[2,64,1024]{2,1,0:T(8,128)(2,1)S(1)}, bf16[2,64,1024]{2,1,0:T(8,128)(2,1)S(1)}, u32[]{:S(2)}, u32[]{:S(2)}) collective-permute-start(bf16[2,64,1024]{2,1,0:T(8,128)(2,1)S(1)} %fusion.145), channel_id=1, source_target_pairs={{0,8},{4,12},{8,16},{12,20},{16,24},{20,28},{24,0},{28,4},{1,9},{5... | collective-permute-start | bytes 786440 | tf_op jit(solution)/shard_map/ppermute | solution.py:73
  196.5 11.3 %collective-permute-start.26 = (bf16[4,2,64,1024]{3,2,1,0:T(8,128)(2,1)}, bf16[4,2,64,1024]{3,2,1,0:T(8,128)(2,1)}, u32[]{:S(2)}, u32[]{:S(2)}) collective-permute-start(bf16[4,2,64,1024]{3,2,1,0:T(8,128)(2,1)} %get-tuple-element.82), channel_id=1, source_target_pairs={{0,4},{4,0},{8,12},{12,8},{16,20},{20,16},{24,28},{28,24},{1,5},{5... | collective-permute-start | bytes 3145736 | tf_op jit(solution)/shard_map/ppermute | solution.py:78
  197.5 153.4 %collective-permute-start.16 = (bf16[2,64,1024]{2,1,0:T(8,128)(2,1)}, bf16[2,64,1024]{2,1,0:T(8,128)(2,1)}, u32[]{:S(2)}, u32[]{:S(2)}) collective-permute-start(bf16[2,64,1024]{2,1,0:T(8,128)(2,1)} %bitcast.60), channel_id=1, source_target_pairs={{0,1},{1,2},{2,3},{3,0},{4,5},{5,6},{6,7},{7,4},{8,9},{9,10},{10,1... | collective-permute-start | bytes 786440 | tf_op jit(solution)/shard_map/ppermute | solution.py:68
  272.5 10.9 %collective-permute-start.27 = (bf16[2,512,128]{2,1,0:T(8,128)(2,1)}, bf16[2,512,128]{2,1,0:T(8,128)(2,1)}, u32[]{:S(2)}, u32[]{:S(2)}) collective-permute-start(bf16[2,512,128]{2,1,0:T(8,128)(2,1)} %get-tuple-element.78), channel_id=1, source_target_pairs={{0,2},{1,3},{2,0},{3,1},{4,6},{5,7},{6,4},{7,5},{8,10},{9,11},{10,... | collective-permute-start | bytes 786440 | tf_op jit(solution)/shard_map/ppermute | solution.py:68
  272.9 14.3 %collective-permute-start.29 = (bf16[2,512,128]{2,1,0:T(8,128)(2,1)}, bf16[2,512,128]{2,1,0:T(8,128)(2,1)}, u32[]{:S(2)}, u32[]{:S(2)}) collective-permute-start(bf16[2,512,128]{2,1,0:T(8,128)(2,1)} %get-tuple-element.79), channel_id=1, source_target_pairs={{0,1},{1,2},{2,3},{3,0},{4,5},{5,6},{6,7},{7,4},{8,9},{9,10},{10,1... | collective-permute-start | bytes 786440 | tf_op jit(solution)/shard_map/ppermute | solution.py:68
  277.3 11.5 %collective-permute-start.28 = (bf16[2,512,128]{2,1,0:T(8,128)(2,1)}, bf16[2,512,128]{2,1,0:T(8,128)(2,1)}, u32[]{:S(2)}, u32[]{:S(2)}) collective-permute-start(bf16[2,512,128]{2,1,0:T(8,128)(2,1)} %get-tuple-element.80), channel_id=1, source_target_pairs={{0,3},{1,0},{2,1},{3,2},{4,7},{5,4},{6,5},{7,6},{8,11},{9,8},{10,9... | collective-permute-start | bytes 786440 | tf_op jit(solution)/shard_map/ppermute | solution.py:68
  312.5 20.5 %collective-permute-start.30 = (bf16[4,2,64,1024]{3,2,1,0:T(8,128)(2,1)S(1)}, bf16[4,2,64,1024]{3,2,1,0:T(8,128)(2,1)S(1)}, u32[]{:S(2)}, u32[]{:S(2)}) collective-permute-start(bf16[4,2,64,1024]{3,2,1,0:T(8,128)(2,1)S(1)} %bitcast.453), channel_id=1, source_target_pairs={{0,4},{4,0},{8,12},{12,8},{16,20},{20,16},{24,28},{28,24},{1,5},{5... | collective-permute-start | bytes 3145736 | tf_op jit(solution)/shard_map/ppermute | solution.py:78
  327.5 23.4 %collective-permute-start.14 = (bf16[2,64,1024]{2,1,0:T(8,128)(2,1)}, bf16[2,64,1024]{2,1,0:T(8,128)(2,1)}, u32[]{:S(2)}, u32[]{:S(2)}) collective-permute-start(bf16[2,64,1024]{2,1,0:T(8,128)(2,1)} %bitcast.58), channel_id=1, source_target_pairs={{0,2},{1,3},{2,0},{3,1},{4,6},{5,7},{6,4},{7,5},{8,10},{9,11},{10,... | collective-permute-start | bytes 786440 | tf_op jit(solution)/shard_map/ppermute | solution.py:68
  (115 other events, 1131.1 us)
Sparse Core Ops, SparseCore 0:
  16.6 50.9 all-gather.1
  207.9 86.7 reduce-scatter.1
